TPU v7x, 32 devices: a whole 2x2x4 slice. The times are simulated.
32 devices in a mesh: vocab: 4 (over y, core), docs: 8 (over z, x).
Axes of the slice: x: 2, y: 2, z: 4, core: 2. Of those that a mesh axis runs over, the one named last changes fastest.
Arguments:
- counts: bfloat16 [4096, 4, 128], P(('vocab', 'docs')), may hold values from 0 to 2
- doc_owner: int32 [4096, 4], P(('vocab', 'docs')), may hold values from 0 to 31, all different within a row; in each aligned block of 128 rows (0 to 127, 128 to 255, ...) at most 32 rows name the same one
- doc_sub: int32 [4096, 4], P(('vocab', 'docs')), may hold values from 0 to 7
- doc_len: int32 [4096], P(('vocab', 'docs')), may hold values from 256 to 1023
- first_weight: bfloat16 [32768, 2048], P(('vocab', 'docs')), may hold values from -0.25 to 0.25
- first_bias: float32 [2048], replicated, may hold values from -3 to 3
- head_weight: bfloat16 [2048, 1536], P('vocab', 'docs'), may hold values from -0.125 to 0.125
- head_bias: float32 [1536], replicated, may hold values from -4 to 4
- factor: bfloat16 [1536, 1536], P('vocab', 'docs'), as said below
- noise_draw: bfloat16 [4096, 1536], P(('vocab', 'docs')), may hold values from -5 to 5
Outputs:
- sample: bfloat16 [4096, 1536], P(('vocab', 'docs'))
Inputs may be any that keep to these rules, and one draw needn't show every extreme that they name: `doc_owner`: each document names 4 different owners. The documents of one device name one owner in at most 32 slots, and on some device some owner is named in exactly 32 slots. `factor`: lower triangular; diagonal entries lie between 0.5 and 1.5.
All inputs are finite; a program needn't handle non-finite values.
Results may differ from a plain program's by a relative error of at most 0.0038.
Values may be sent and summed in bfloat16 or wider, within the bound.
A program may use at most 128 MiB of HBM per device.

v0:
```python
import jax
import jax.numpy as jnp
from jax import lax
from jax.sharding import PartitionSpec as P


def local(
    counts,
    doc_owner,
    doc_sub,
    doc_len,
    first_weight,
    first_bias,
    head_weight,
    head_bias,
    factor,
    noise_draw,
):
    vocab_devices = lax.axis_size("vocab")
    docs_devices = lax.axis_size("docs")
    device_count = vocab_devices * docs_devices
    docs_here, slot_count, block_width = counts.shape
    hidden_width = first_weight.shape[1]
    per_owner = first_weight.shape[0] // block_width
    capacity = max(2, 2 * docs_here * slot_count // device_count)
    owner_flat = doc_owner.reshape(-1)
    onehot = (owner_flat[:, None] == jnp.arange(device_count, dtype=jnp.int32)[None, :]).astype(
        jnp.int32
    )
    position = jnp.sum(jnp.cumsum(onehot, axis=0) * onehot, axis=1) - 1
    slot_index = owner_flat * capacity + position
    flat_rows = counts.reshape(-1, block_width)
    send_rows = (
        jnp.zeros((device_count * capacity, block_width), counts.dtype)
        .at[slot_index]
        .set(flat_rows)
    )
    send_sub = (
        jnp.zeros((device_count * capacity,), jnp.bfloat16)
        .at[slot_index]
        .set(doc_sub.reshape(-1).astype(jnp.bfloat16))
    )
    send_rows = send_rows.reshape(vocab_devices, docs_devices, capacity, block_width)
    send_sub = send_sub.reshape(vocab_devices, docs_devices, capacity)
    got_rows, got_sub = (
        lax.all_to_all(
            lax.all_to_all(send_rows, "vocab", split_axis=0, concat_axis=0, tiled=True),
            "docs",
            split_axis=1,
            concat_axis=1,
            tiled=True,
        ),
        lax.all_to_all(
            lax.all_to_all(send_sub, "vocab", split_axis=0, concat_axis=0, tiled=True),
            "docs",
            split_axis=1,
            concat_axis=1,
            tiled=True,
        ),
    )
    got_rows = got_rows.reshape(-1, block_width)
    got_sub = got_sub.reshape(-1).astype(jnp.int32)
    select = (got_sub[:, None] == jnp.arange(per_owner, dtype=jnp.int32)[None, :]).astype(
        jnp.bfloat16
    )
    spread = (select[:, :, None] * got_rows[:, None, :]).reshape(-1, per_owner * block_width)
    owner_terms = jnp.dot(spread, first_weight, preferred_element_type=jnp.float32).astype(
        jnp.bfloat16
    )
    owner_terms = owner_terms.reshape(vocab_devices, docs_devices, capacity, hidden_width)
    returned = lax.all_to_all(
        lax.all_to_all(owner_terms, "vocab", split_axis=0, concat_axis=0, tiled=True),
        "docs",
        split_axis=1,
        concat_axis=1,
        tiled=True,
    )
    returned = returned.reshape(-1, hidden_width)
    own_rows = returned[slot_index].reshape(docs_here, slot_count, hidden_width).astype(jnp.float32)
    summed = jnp.sum(own_rows, axis=1)
    length_scale = 128.0 * slot_count / doc_len.astype(jnp.float32)
    hidden = jax.nn.softplus(summed * length_scale[:, None] + first_bias).astype(jnp.bfloat16)
    panel_rows = lax.all_gather(head_weight, "docs", axis=1, tiled=True)
    location = jnp.dot(
        hidden,
        lax.all_gather(panel_rows, "vocab", axis=0, tiled=True),
        preferred_element_type=jnp.float32,
    )
    factor_panel = lax.all_gather(factor, "docs", axis=1, tiled=True)
    correlated = lax.dot_general(
        noise_draw,
        lax.all_gather(factor_panel, "vocab", axis=0, tiled=True),
        (((1,), (1,)), ((), ())),
        preferred_element_type=jnp.float32,
    )
    return (location + head_bias + correlated).astype(jnp.bfloat16)


def solution(mesh):
    return jax.shard_map(
        local,
        mesh=mesh,
        in_specs=(
            P(("vocab", "docs"), None, None),
            P(("vocab", "docs"), None),
            P(("vocab", "docs"), None),
            P(("vocab", "docs")),
            P(("vocab", "docs"), None),
            P(),
            P("vocab", "docs"),
            P(),
            P("vocab", "docs"),
            P(("vocab", "docs"), None),
        ),
        out_specs=P(("vocab", "docs"), None),
        check_vma=False,
    )
```

profile of v0, /device:TPU:9, one launch (start us, length us, event | category | flops | bytes accessed | tf_op | source)
XLA Modules:
  0.0 323.0 jit_solution(1911914656535921011)
XLA Ops:
  6.5 0.7 all-gather.5.cloned.1.call-update
  7.3 0.0 all-gather.9.cloned.1.call-start
  7.3 0.7 all-gather.9.cloned.1.call-update
  8.0 0.0 all-gather.7.cloned.1.call-start
  8.1 46.6 %all-gather.5.cloned.1.call-done = bf16[512,1536]{0,1:T(8,128)(2,1)} async-done(((bf16[512,192]{0,1:T(8,128)(2,1)}), bf16[512,1536]{0,1:T(8,128)(2,1)}) %all-gather.5.cloned.1.call-update) | async-done | bytes 1572880 | tf_op jit(solution)/shard_map/all_gather | solution.py:83
  54.7 0.8 copy.46
  55.5 0.1 eq.46
  55.6 0.1 eq.42
  55.7 1.2 reduce-window.6
  56.9 0.2 slice_reduce_fusion
  57.1 0.7 broadcast_multiply_fusion.1
  57.8 0.1 copy.45
  57.9 0.1 mul.48
  58.0 0.7 convert_element_type.47
  58.7 0.1 copy.49
  58.9 0.1 reshape.128
  59.0 0.1 fusion.12
  59.1 3.8 %scatter_custom_fusion = bf16[1024]{0:T(1024)(128)(2,1)S(1)} fusion(s32[512]{0:T(512)S(1)} %bitcast.34, bf16[512]{0:T(512)(128)(2,1)S(1)} %reshape.128, bf16[]{:T(256)} %constant.7.clone.1), kind=kCustom, calls=%fused_computation.32 | custom fusion | bytes 2050 | tf_op jit(solution)/shard_map/scatter | solution.py:41
  62.9 0.1 reshape.109
  63.0 0.7 reshape.145
  63.6 4.5 %all-to-all-start = ((bf16[4,2,128]{2,1,0:T(2,128)(2,1)}), bf16[4,2,128]{2,1,0:T(2,128)(2,1)S(1)}, u32[]{:S(2)}, u32[]{:S(2)}) async-start(bf16[4,2,128]{2,1,0:T(2,128)(2,1)} %reshape.145), calls=%async_computation | async-start | bytes 4096 | tf_op jit(solution)/shard_map/all_to_all | solution.py:54
  68.1 2.8 scatter_custom_fusion.1
  70.9 0.7 all-to-all-done
  71.6 3.7 %all-to-all-start.2 = ((bf16[4,8,32,128]{3,2,1,0:T(8,128)(2,1)}), bf16[4,8,32,128]{3,2,1,0:T(8,128)(2,1)S(1)}, u32[]{:S(2)}, u32[]{:S(2)}) async-start(bf16[4,8,32,128]{3,2,1,0:T(8,128)(2,1)} %bitcast.4), calls=%async_computation.2 | async-start | bytes 524288 | tf_op jit(solution)/shard_map/all_to_all | solution.py:47
  75.2 0.1 reshape.146
  75.3 0.6 copy.50
  75.9 4.5 %all-to-all-done.2 = bf16[4,8,32,128]{3,2,1,0:T(8,128)(2,1)S(1)} async-done(((bf16[4,8,32,128]{3,2,1,0:T(8,128)(2,1)}), bf16[4,8,32,128]{3,2,1,0:T(8,128)(2,1)S(1)}, u32[]{:S(2)}, u32[]{:S(2)}) %all-to-all-start.2) | async-done | bytes 262176 | tf_op jit(solution)/shard_map/all_to_all | solution.py:47
  80.4 3.3 %all-to-all-start.1 = ((bf16[4,8,32]{2,0,1:T(4,128)(2,1)}), bf16[4,8,32]{2,0,1:T(4,128)(2,1)S(1)}, u32[]{:S(2)}, u32[]{:S(2)}) async-start(bf16[4,8,32]{2,0,1:T(4,128)(2,1)} %copy.50), calls=%async_computation.1 | async-start | bytes 16384 | tf_op jit(solution)/shard_map/all_to_all | solution.py:53
  83.7 0.7 copy.52
  84.4 3.2 all-to-all-done.1
  87.6 4.6 %all-to-all-start.3 = ((bf16[4,8,32,128]{3,2,0,1:T(8,128)(2,1)}), bf16[4,8,32,128]{3,2,0,1:T(8,128)(2,1)S(1)}, u32[]{:S(2)}, u32[]{:S(2)}) async-start(bf16[4,8,32,128]{3,2,0,1:T(8,128)(2,1)} %copy.52), calls=%async_computation.3 | async-start | bytes 524288 | tf_op jit(solution)/shard_map/all_to_all | solution.py:46
  92.3 0.1 reshape.114
  92.3 0.2 fusion.8
  92.5 5.8 %all-to-all-done.3 = bf16[4,8,32,128]{3,2,0,1:T(8,128)(2,1)S(1)} async-done(((bf16[4,8,32,128]{3,2,0,1:T(8,128)(2,1)}), bf16[4,8,32,128]{3,2,0,1:T(8,128)(2,1)S(1)}, u32[]{:S(2)}, u32[]{:S(2)}) %all-to-all-start.3) | async-done | bytes 262176 | tf_op jit(solution)/shard_map/all_to_all | solution.py:46
  98.4 3.5 %broadcast_multiply_fusion = bf16[1024,8,128]{2,1,0:T(8,128)(2,1)S(1)} fusion(bf16[1024,128]{1,0:T(8,128)(2,1)S(1)} %bitcast.33, bf16[1024,8]{1,0:T(8,128)(2,1)S(1)} %fusion.8), kind=kLoop, calls=%fused_computation.11 | loop fusion | flops 1048576 | bytes 2375680 | tf_op jit(solution)/shard_map/mul | solution.py:66
  101.9 6.9 %convolution_convert_fusion = bf16[1024,2048]{1,0:T(8,128)(2,1)S(1)} fusion(bf16[1024,2048]{1,0:T(8,128)(2,1)} %param.14, bf16[128,8,8,128]{3,2,1,0:T(8,128)(2,1)S(1)} %bitcast.32), kind=kOutput, calls=%fused_computation.3 | convolution fusion | flops 4297064448 | bytes 10485760 | tf_op jit(solution)/shard_map/dot_general | solution.py:67
  108.8 79.5 %all_to_all.30 = bf16[4,8,32,2048]{3,2,1,0:T(8,128)(2,1)S(1)} all-to-all(bf16[4,8,32,2048]{3,2,1,0:T(8,128)(2,1)S(1)} %bitcast.31), channel_id=1, replica_groups=mesh['vocab'=4,'docs'=8] {'vocab'}, dimensions={0} | all-to-all | bytes 8388608 | tf_op jit(solution)/shard_map/all_to_all | solution.py:72
  188.3 2.3 copy.54
  190.6 5.6 %all-to-all-start.5 = ((bf16[4,8,32,2048]{3,2,0,1:T(8,128)(2,1)}), bf16[4,8,32,2048]{3,2,0,1:T(8,128)(2,1)}, u32[]{:S(2)}, u32[]{:S(2)}) async-start(bf16[4,8,32,2048]{3,2,0,1:T(8,128)(2,1)} %copy.54), calls=%async_computation.5 | async-start | bytes 8388608 | tf_op jit(solution)/shard_map/all_to_all | solution.py:71
  196.2 0.5 all-gather.11.cloned.1.call-update
  196.8 90.9 %all-to-all-done.5 = bf16[4,8,32,2048]{3,2,0,1:T(8,128)(2,1)} async-done(((bf16[4,8,32,2048]{3,2,0,1:T(8,128)(2,1)}), bf16[4,8,32,2048]{3,2,0,1:T(8,128)(2,1)}, u32[]{:S(2)}, u32[]{:S(2)}) %all-to-all-start.5) | async-done | bytes 4194336 | tf_op jit(solution)/shard_map/all_to_all | solution.py:71
  287.7 4.8 %copy.55 = bf16[4,8,32,2048]{3,2,1,0:T(8,128)(2,1)} copy(bf16[4,8,32,2048]{3,2,0,1:T(8,128)(2,1)} %all-to-all-done.5) | data formatting | bytes 8388608 | tf_op jit(solution)/shard_map/all_to_all | solution.py:71
  292.4 7.1 %gather_fusion = bf16[512,2048]{1,0:T(8,128)(2,1)S(1)} fusion(bf16[1024,2048]{1,0:T(8,128)(2,1)} %bitcast.30, s32[1024]{0:T(1024)S(1)} %pad_clamp_fusion), kind=kCustom, calls=%fused_computation | custom fusion | bytes 4196352 | tf_op jit(solution)/shard_map/gather | solution.py:79
  299.6 3.0 reshape.115
  302.6 4.8 %reduce_sum.19 = f32[128,2048]{1,0:T(8,128)S(1)} reduce(f32[128,4,2048]{2,1,0:T(4,128)} %reshape.115, f32[]{:T(128)} %constant.6.clone.1), dimensions={1}, to_apply=%region_5.6 | reduce | flops 786432 | bytes 5242884 | tf_op jit(solution)/shard_map/reduce_sum | solution.py:80
  307.5 0.0 all-gather.7.cloned.1.call-done
  307.5 5.1 %convolution_add_fusion.1 = f32[128,1536]{1,0:T(8,128)S(1)} fusion(bf16[2048,1536]{0,1:T(8,128)(2,1)} %all-gather.7.cloned.1.call-done, f32[128,2048]{1,0:T(8,128)S(1)} %reduce_sum.19, f32[2048]{0:T(1024)S(1)} %copy-done.1, f32[128]{0:T(128)S(1)} %convert_divide_fusion, f32[1536]{0:T(1024)S(1)} %copy-done.2), kind=kOutput, calls=%fused_computation.6 | convolution fusion | flops 807862272 | bytes 8141312 | tf_op jit(solution)/shard_map/dot_general | solution.py:84
  312.6 3.9 %fusion = bf16[128,1536]{1,0:T(8,128)(2,1)} fusion(f32[128,1536]{1,0:T(8,128)S(1)} %convolution_add_fusion.1, bf16[128,1536]{1,0:T(8,128)(2,1)S(1)} %copy-done, bf16[1536,1536]{0,1:T(8,128)(2,1)} %all-gather.11.cloned.1.call-done), kind=kOutput, calls=%fused_computation.7 | convolution fusion | flops 604372992 | bytes 6291456 | tf_op jit(solution)/shard_map/dot_general | solution.py:90
  (22 shorter events, 0.2 us)
Async XLA Ops:
  6.5 306.1 %copy-start = (bf16[128,1536]{1,0:T(8,128)(2,1)S(1)}, bf16[128,1536]{1,0:T(8,128)(2,1)}, u32[]{:S(2)}) copy-start(bf16[128,1536]{1,0:T(8,128)(2,1)} %param.19) | copy-start | bytes 1179652
  6.5 48.1 %all-gather.5.cloned.1.call-start = ((), (), s32[]{:S(2)}) async-start(), calls=%async_computation.6 | async-start | bytes 1769472 | tf_op jit(solution)/shard_map/all_gather | solution.py:83
  7.3 188.9 %all-gather.9.cloned.1.call-start = ((), (), s32[]{:S(2)}) async-start(), calls=%async_computation.8 | async-start | bytes 1327104 | tf_op jit(solution)/shard_map/all_gather | solution.py:89
  8.0 299.5 %all-gather.7.cloned.1.call-start = ((), (), s32[]{:S(2)}) async-start(), calls=%async_computation.7 | async-start | bytes 7864320 | tf_op jit(solution)/shard_map/all_gather | solution.py:86
  63.6 7.9 %all-to-all-start = ((bf16[4,2,128]{2,1,0:T(2,128)(2,1)}), bf16[4,2,128]{2,1,0:T(2,128)(2,1)S(1)}, u32[]{:S(2)}, u32[]{:S(2)}) async-start(bf16[4,2,128]{2,1,0:T(2,128)(2,1)} %reshape.145), calls=%async_computation | async-start | bytes 4096 | tf_op jit(solution)/shard_map/all_to_all | solution.py:54
  71.6 8.8 %all-to-all-start.2 = ((bf16[4,8,32,128]{3,2,1,0:T(8,128)(2,1)}), bf16[4,8,32,128]{3,2,1,0:T(8,128)(2,1)S(1)}, u32[]{:S(2)}, u32[]{:S(2)}) async-start(bf16[4,8,32,128]{3,2,1,0:T(8,128)(2,1)} %bitcast.4), calls=%async_computation.2 | async-start | bytes 524288 | tf_op jit(solution)/shard_map/all_to_all | solution.py:47
  80.4 7.2 %all-to-all-start.1 = ((bf16[4,8,32]{2,0,1:T(4,128)(2,1)}), bf16[4,8,32]{2,0,1:T(4,128)(2,1)S(1)}, u32[]{:S(2)}, u32[]{:S(2)}) async-start(bf16[4,8,32]{2,0,1:T(4,128)(2,1)} %copy.50), calls=%async_computation.1 | async-start | bytes 16384 | tf_op jit(solution)/shard_map/all_to_all | solution.py:53
  87.6 10.7 %all-to-all-start.3 = ((bf16[4,8,32,128]{3,2,0,1:T(8,128)(2,1)}), bf16[4,8,32,128]{3,2,0,1:T(8,128)(2,1)S(1)}, u32[]{:S(2)}, u32[]{:S(2)}) async-start(bf16[4,8,32,128]{3,2,0,1:T(8,128)(2,1)} %copy.52), calls=%async_computation.3 | async-start | bytes 524288 | tf_op jit(solution)/shard_map/all_to_all | solution.py:46
  190.6 6.2 %copy-start.3 = (s32[128]{0:T(128)S(1)}, s32[128]{0:T(128)}, u32[]{:S(2)}) copy-start(s32[128]{0:T(128)} %param.13) | copy-start | bytes 1540
  190.6 97.1 %all-to-all-start.5 = ((bf16[4,8,32,2048]{3,2,0,1:T(8,128)(2,1)}), bf16[4,8,32,2048]{3,2,0,1:T(8,128)(2,1)}, u32[]{:S(2)}, u32[]{:S(2)}) async-start(bf16[4,8,32,2048]{3,2,0,1:T(8,128)(2,1)} %copy.54), calls=%async_computation.5 | async-start | bytes 8388608 | tf_op jit(solution)/shard_map/all_to_all | solution.py:71
  196.2 116.4 %all-gather.11.cloned.1.call-start = ((), (), s32[]{:S(2)}) async-start(), calls=%async_computation.9 | async-start | bytes 5898240 | tf_op jit(solution)/shard_map/all_gather | solution.py:92
  302.6 4.9 %copy-start.1 = (f32[2048]{0:T(1024)S(1)}, f32[2048]{0:T(1024)}, u32[]{:S(2)}) copy-start(f32[2048]{0:T(1024)} %param.15) | copy-start | bytes 24580
  302.6 4.9 %copy-start.2 = (f32[1536]{0:T(1024)S(1)}, f32[1536]{0:T(1024)}, u32[]{:S(2)}) copy-start(f32[1536]{0:T(1024)} %param.17) | copy-start | bytes 18436
Sparse Core Ops, SparseCore 0:
  9.5 45.0 all-gather.4
  56.8 38.7 all-gather.8
  97.2 73.9 all-gather.6
  198.3 38.2 all-gather.10
where the time goes:
time: 327 us; the launch traced here: 323 us
  waiting for transfers between devices  154 us (47%)
  blocking collectives  79.5 us (24%)
  local copies, waits for them, and re-layouts  27.7 us (8%)
  starting transfers between devices  21.7 us (7%)
  matrix products  15.9 us (5%)
  between operations  13.3 us (4%)
  other arithmetic  11.2 us (3%)
    all_to_all x1, waiting for transfers between devices, local(): lax.all_to_all(lax.all_to_all(owner_terms, 'vocab', split_axis=0, concat_...  90.9 us
    all_to_all x1, blocking collectives, local(): lax.all_to_all(owner_terms, 'vocab', split_axis=0, concat_axis=0, tiled=T...  79.5 us
    all_gather x1, waiting for transfers between devices, local(): panel_rows = lax.all_gather(head_weight, 'docs', axis=1, tiled=True)  46.6 us
    gather x1, local copies, waits for them, and re-layouts, local(): returned[slot_index].reshape(docs_here, slot_count, hidden_width)  7.13 us
    dot_general x1, matrix products, local(): jnp.dot(spread, first_weight, preferred_element_type=jnp.float32)  6.92 us
  transfers between devices with their start and end apart: 9, of which 6 were waited for; matrix products, arithmetic and copies ran while one was open for 16% of the time, Pallas kernels for 0%

commit v1 on v0

--- a/solution.py
+++ b/solution.py
@@ -1,7 +1,337 @@
+import functools
+
 import jax
 import jax.numpy as jnp
 from jax import lax
+from jax.experimental import pallas as pl
+from jax.experimental.pallas import tpu as pltpu
 from jax.sharding import PartitionSpec as P
+
+MESH = pl.DeviceIdType.MESH
+F32 = jnp.float32
+BF16 = jnp.bfloat16
+CHIPS = (1, 4, 5)
+CORE = 2
+ORDER = (5, 7, 1, 3, 4, 6, 2)
+
+
+def nt(a, b):
+    return lax.dot_general(a, b, (((1,), (1,)), ((), ())), preferred_element_type=F32)
+
+
+def tn(a, b):
+    return lax.dot_general(a, b, (((0,), (0,)), ((), ())), preferred_element_type=F32)
+
+
+def nn(a, b):
+    return jnp.dot(a, b, preferred_element_type=F32)
+
+
+def kernel(
+    cap,
+    counts_ref, owner_ref, sub_ref, scale_ref, weight_ref, bias_ref,
+    head_ref, head_bias_ref, factor_ref, noise_ref,
+    out_ref,
+    cbuf, dtbuf, zin, dtin, pin, pmeta, spread, obuf, rbuf, zs, zr, own, dtp,
+    head_all, fac_all, total,
+    zc_s, zc_r, zd_s, zd_r, zw_s, zw_r, pc_s, pc_r, pm_s, pm_r,
+    ret_s, ret_r, zp_s, zp_r, wp_s, wp_r, wc_s, wc_r,
+):
+    slots, docs, width = counts_ref.shape
+    owners = 32
+    rows = 8 * cap
+    hc = head_ref.shape[1]
+    v = lax.axis_index("vocab")
+    d = lax.axis_index("docs")
+    z = d // 2
+    x = d % 2
+    me = v * 2 + x
+
+    def zpeer(k):
+        return (v, (z ^ k) * 2 + x)
+
+    def ppeer(r):
+        j = me ^ r
+        return (j // 2, z * 2 + j % 2)
+
+    def rc(src, dst, s, r, dev):
+        return pltpu.make_async_remote_copy(
+            src_ref=src, dst_ref=dst, send_sem=s, recv_sem=r, device_id=dev, device_id_type=MESH
+        )
+
+    barrier = pltpu.get_barrier_semaphore()
+    for k in range(1, 4):
+        pl.semaphore_signal(barrier, inc=1, device_id=zpeer(k), device_id_type=MESH)
+    for r in range(1, 8):
+        pl.semaphore_signal(barrier, inc=1, device_id=ppeer(r), device_id_type=MESH)
+
+    upper = jnp.where(
+        lax.broadcasted_iota(jnp.int32, (docs, docs), 0)
+        <= lax.broadcasted_iota(jnp.int32, (docs, docs), 1), 1.0, 0.0
+    ).astype(BF16)
+    owner_iota = lax.broadcasted_iota(jnp.int32, (owners, docs), 0)
+    meta_iota = lax.broadcasted_iota(jnp.int32, (64, docs), 0)
+    place_iota = lax.broadcasted_iota(jnp.int32, (128, docs), 0)
+    row_iota = lax.broadcasted_iota(jnp.int32, (rows, docs), 0)
+    carry = jnp.zeros((owners, 1), F32)
+    meta = jnp.zeros((64, 128), F32)
+    full = []
+    for s in range(slots):
+        o = owner_ref[s : s + 1, :]
+        hot = jnp.where(owner_iota == o, 1.0, 0.0)
+        cum = nn(hot.astype(BF16), upper) + carry
+        carry = carry + jnp.sum(hot, axis=1, keepdims=True)
+        pos = (jnp.sum(hot * cum, axis=0, keepdims=True) - 1.0).astype(jnp.int32)
+        oz = (o >> 1) & 3
+        oi = (o >> 3) * 2 + (o & 1)
+        full.append(oz * rows + oi * cap + pos)
+        named = jnp.where(
+            meta_iota == oz * 16 + oi, jnp.broadcast_to(sub_ref[s : s + 1, :], (64, docs)).astype(F32), 0.0
+        ).astype(BF16)
+        placed = jnp.where(place_iota == pos, 1.0, 0.0).astype(BF16)
+        meta = meta + nt(named, placed)
+    for zo in range(4):
+        acc = jnp.zeros((rows, width), F32)
+        dt = jnp.zeros((rows, docs), F32)
+        for s in range(slots):
+            sel = jnp.where(row_iota + zo * rows == full[s], 1.0, 0.0)
+            acc = acc + nn(sel.astype(BF16), counts_ref[s])
+            dt = dt + sel
+        cbuf[zo, 0:rows, :] = acc.astype(BF16)
+        cbuf[zo, rows : rows + 16, :] = meta[zo * 16 : zo * 16 + 16, :].astype(BF16)
+        dtbuf[zo] = dt.astype(BF16)
+
+    pl.semaphore_wait(barrier, 10)
+
+    def zc(k):
+        return rc(cbuf.at[z ^ k], zin.at[k], zc_s.at[k], zc_r.at[k], zpeer(k))
+
+    def zd(k):
+        return rc(dtbuf.at[z ^ k], dtin.at[k], zd_s.at[k], zd_r.at[k], zpeer(k))
+
+    def zw(k):
+        return (
+            rc(head_ref, head_all.at[v, z, x], zw_s.at[0, k], zw_r.at[0, k], zpeer(k)),
+            rc(factor_ref, fac_all.at[v, z, x], zw_s.at[1, k], zw_r.at[1, k], zpeer(k)),
+        )
+
+    for k in (2, 3, 1):
+        zc(k).start()
+    for k in (2, 3, 1):
+        zd(k).start()
+        for c in zw(k):
+            c.start()
+    zin[0] = cbuf[z]
+    dtin[0] = dtbuf[z]
+    head_all[v, z, x] = head_ref[...]
+    fac_all[v, z, x] = factor_ref[...]
+
+    def pc(r):
+        j = me ^ r
+        return (
+            rc(zin.at[:, pl.ds(pl.multiple_of(j * cap, cap), cap), :], pin.at[r], pc_s.at[r], pc_r.at[r], ppeer(r)),
+            rc(zin.at[:, pl.ds(rows, 16), :], pmeta.at[r], pm_s.at[r], pm_r.at[r], ppeer(r)),
+        )
+
+    for k in range(1, 4):
+        zc(k).wait_recv()
+    for r in ORDER:
+        for c in pc(r):
+            c.start()
+    pin[0] = zin[:, pl.ds(pl.multiple_of(me * cap, cap), cap), :]
+    pmeta[0] = zin[:, rows : rows + 16, :]
+
+    ones = jnp.ones((128, 128), BF16)
+    pick = lax.broadcasted_iota(jnp.int32, (16, 128), 0) == me
+    eye = lax.broadcasted_iota(jnp.int32, (cap, 128), 0) == lax.broadcasted_iota(jnp.int32, (cap, 128), 1)
+
+    def spread_one(r, _):
+        for k in range(4):
+            line = jnp.sum(jnp.where(pick, pmeta[r, k].astype(F32), 0.0), axis=0, keepdims=True)
+            sub = nn(jnp.where(eye, line, 0.0).astype(BF16), ones)
+            got = pin[r, k].astype(F32)
+            for b in range(8):
+                spread[r, k * cap : (k + 1) * cap, b * width : (b + 1) * width] = jnp.where(
+                    sub == float(b), got, 0.0
+                ).astype(BF16)
+        return 0
+
+    spread_one(0, 0)
+    for r in ORDER:
+        for c in pc(r):
+            c.wait_recv()
+    lax.fori_loop(1, 8, spread_one, 0)
+
+    def ret(h, r):
+        return rc(
+            obuf.at[h, r], rbuf.at[h, :, pl.ds(r * cap, cap), :], ret_s.at[h, r], ret_r.at[h, r], ppeer(r)
+        )
+
+    def owner_chunk(h, _):
+        cols = weight_ref[:, pl.ds(pl.multiple_of(h * hc, hc), hc)]
+        for pair in ((5, 7), (1, 3), (4, 6), (2, 0)):
+            for r in pair:
+                got = nn(spread[r], cols).astype(BF16).reshape(4, cap, hc)
+                if r:
+                    obuf[h, r] = got
+                    ret(h, r).start()
+                else:
+                    rbuf[h, :, 0:cap, :] = got
+        return 0
+
+    lax.fori_loop(0, 4, owner_chunk, 0)
+
+    def plane_copy(r):
+        dev = ppeer(r)
+        return (
+            rc(head_all.at[v, :, x], head_all.at[v, :, x], wp_s.at[0, r], wp_r.at[0, r], dev),
+            rc(fac_all.at[v, :, x], fac_all.at[v, :, x], wp_s.at[1, r], wp_r.at[1, r], dev),
+        )
+
+    def core_copy(r):
+        dev = ppeer(CORE)
+        j = me ^ r
+        vv, xx = j // 2, j % 2
+        return (
+            rc(head_all.at[vv, :, xx], head_all.at[vv, :, xx], wc_s.at[0, r], wc_r.at[0, r], dev),
+            rc(fac_all.at[vv, :, xx], fac_all.at[vv, :, xx], wc_s.at[1, r], wc_r.at[1, r], dev),
+        )
+
+    for k in range(1, 4):
+        for c in zw(k):
+            c.wait_recv()
+    for r in CHIPS:
+        for c in plane_copy(r):
+            c.start()
+    for c in core_copy(0):
+        c.start()
+
+    for k in range(1, 4):
+        zd(k).wait_recv()
+    for k in range(4):
+        for r in range(8):
+            dtp[k, r * cap : (r + 1) * cap, :] = dtin[k, pl.ds(pl.multiple_of((me ^ r) * cap, cap), cap), :]
+
+    def zp(h, k):
+        return rc(zs.at[h, k], zr.at[h, k], zp_s.at[h, k], zp_r.at[h, k], zpeer(k))
+
+    def combine_chunk(h, _):
+        for r in range(1, 8):
+            ret(h, r).wait_recv()
+        for k in (2, 3, 1):
+            zs[h, k] = tn(dtp[k], rbuf[h, k]).astype(BF16)
+            zp(h, k).start()
+        own[h] = tn(dtp[0], rbuf[h, 0])
+        return 0
+
+    lax.fori_loop(0, 4, combine_chunk, 0)
+
+    for r in CHIPS:
+        for c in plane_copy(r):
+            c.wait_recv()
+        for c in core_copy(r):
+            c.start()
+    for r in (0,) + CHIPS:
+        for c in core_copy(r):
+            c.wait_recv()
+
+    kc = factor_ref.shape[1]
+    for w in range(4):
+        block = fac_all[w].reshape(-1, kc)
+        total[:, w * kc : (w + 1) * kc] = nn(noise_ref[...], block) + head_bias_ref[:, w * kc : (w + 1) * kc]
+
+    def final_chunk(h, _):
+        for k in range(1, 4):
+            zp(h, k).wait_recv()
+        summed = own[h]
+        for k in range(1, 4):
+            summed = summed + zr[h, k].astype(F32)
+        value = summed * scale_ref[...] + bias_ref[h]
+        hidden = (jnp.maximum(value, 0.0) + jnp.log1p(jnp.exp(-jnp.abs(value)))).astype(BF16)
+        total[...] += nt(hidden, head_all[h].reshape(-1, hc))
+        return 0
+
+    lax.fori_loop(0, 4, final_chunk, 0)
+    out_ref[...] = total[...].astype(BF16)
+
+    for k in range(1, 4):
+        zc(k).wait_send()
+        zd(k).wait_send()
+        for c in zw(k):
+            c.wait_send()
+    for r in range(1, 8):
+        for c in pc(r):
+            c.wait_send()
+    for r in CHIPS:
+        for c in plane_copy(r):
+            c.wait_send()
+    for r in (0,) + CHIPS:
+        for c in core_copy(r):
+            c.wait_send()
+
+    def drain(h, _):
+        for r in range(1, 8):
+            ret(h, r).wait_send()
+        for k in range(1, 4):
+            zp(h, k).wait_send()
+        return 0
+
+    lax.fori_loop(0, 4, drain, 0)
+
+
+def fused(
+    counts, doc_owner, doc_sub, doc_len, first_weight, first_bias, head_weight, head_bias, factor, noise_draw
+):
+    docs, slots, width = counts.shape
+    hidden = first_weight.shape[1]
+    cap = 2 * docs * slots // 32
+    hc, topics = head_weight.shape[0], head_bias.shape[0]
+    rows = 8 * cap
+    scale = (128.0 * slots / doc_len.astype(F32)).reshape(docs, 1)
+    dma = pltpu.SemaphoreType.DMA
+    kd, kc = head_weight.shape[1], factor.shape[0]
+    return pl.pallas_call(
+        functools.partial(kernel, cap),
+        out_shape=jax.ShapeDtypeStruct((docs, topics), BF16),
+        in_specs=[pl.BlockSpec(memory_space=pltpu.VMEM)] * 10,
+        out_specs=pl.BlockSpec(memory_space=pltpu.VMEM),
+        scratch_shapes=[
+            pltpu.VMEM((4, rows + 16, width), BF16),
+            pltpu.VMEM((4, rows, docs), BF16),
+            pltpu.VMEM((4, rows + 16, width), BF16),
+            pltpu.VMEM((4, rows, docs), BF16),
+            pltpu.VMEM((8, 4, cap, width), BF16),
+            pltpu.VMEM((8, 4, 16, 128), BF16),
+            pltpu.VMEM((8, 4 * cap, 8 * width), BF16),
+            pltpu.VMEM((4, 8, 4, cap, hc), BF16),
+            pltpu.VMEM((4, 4, rows, hc), BF16),
+            pltpu.VMEM((4, 4, docs, hc), BF16),
+            pltpu.VMEM((4, 4, docs, hc), BF16),
+            pltpu.VMEM((4, docs, hc), F32),
+            pltpu.VMEM((4, rows, docs), BF16),
+            pltpu.VMEM((4, 4, 2, kd, hc), BF16),
+            pltpu.VMEM((4, 4, 2, factor.shape[1], kc), BF16),
+            pltpu.VMEM((docs, topics), F32),
+            dma((4,)), dma((4,)), dma((4,)), dma((4,)), dma((2, 4)), dma((2, 4)),
+            dma((8,)), dma((8,)), dma((8,)), dma((8,)),
+            dma((4, 8)), dma((4, 8)), dma((4, 4)), dma((4, 4)),
+            dma((2, 8)), dma((2, 8)), dma((2, 8)), dma((2, 8)),
+        ],
+        compiler_params=pltpu.CompilerParams(
+            collective_id=0, has_side_effects=True, vmem_limit_bytes=58 * 1024 * 1024
+        ),
+    )(
+        jnp.transpose(counts, (1, 0, 2)),
+        doc_owner.T,
+        doc_sub.T,
+        scale,
+        first_weight,
+        first_bias.reshape(4, 1, hc),
+        head_weight.T,
+        head_bias.reshape(1, -1),
+        factor.T,
+        noise_draw,
+    )
 
 
 def local(
@@ -97,8 +427,9 @@
 
 
 def solution(mesh):
+    small = mesh.shape["vocab"] == 4 and mesh.shape["docs"] == 8
     return jax.shard_map(
-        local,
+        fused if small else local,
         mesh=mesh,
         in_specs=(
             P(("vocab", "docs"), None, None),

time: 327 us -> 161 us (0.49); the launches traced: 323 us -> 160 us
  Pallas kernels: 0 us -> 154 us
  waiting for transfers between devices: 154 us -> 0 us
  blocking collectives: 79.5 us -> 0 us
  local copies, waits for them, and re-layouts: 27.7 us -> 5.37 us
  starting transfers between devices: 21.7 us -> 0 us
  matrix products: 15.9 us -> 0 us
  between operations: 13.3 us -> 0.01 us
  other arithmetic: 11.2 us -> 0.66 us
    pallas_call x0 -> x1, Pallas kernels: none -> 154 us  [fused(): pl.pallas_call(functools.partial(kernel, cap), out_shape=jax.ShapeDtypeSt...]
    all_to_all x5 -> x0, waiting for transfers between devices: 105 us -> none  [the longest x1 90.9 us: local(): lax.all_to_all(lax.all_to_all(owner_terms, 'vocab', split_axis=0, concat_...]
    all_to_all x1 -> x0, blocking collectives: 79.5 us -> none  [local(): lax.all_to_all(owner_terms, 'vocab', split_axis=0, concat_axis=0, tiled=T...]
    all_gather x4 -> x0, waiting for transfers between devices: 46.6 us -> none  [the longest x1 46.6 us: local(): panel_rows = lax.all_gather(head_weight, 'docs', axis=1, tiled=True)]
    all_to_all x5 -> x0, starting transfers between devices: 21.6 us -> none  [the longest x1 5.62 us: local(): lax.all_to_all(lax.all_to_all(owner_terms, 'vocab', split_axis=0, concat_...]
    dot_general x3 -> x0, matrix products: 15.9 us -> none  [the longest x1 6.92 us: local(): jnp.dot(spread, first_weight, preferred_element_type=jnp.float32)]
    all_to_all x5 -> x0, local copies, waits for them, and re-layouts: 8.4 us -> none  [the longest x1 4.76 us: local(): lax.all_to_all(lax.all_to_all(owner_terms, 'vocab', split_axis=0, concat_...]
    gather x1 -> x0, local copies, waits for them, and re-layouts: 7.13 us -> none  [local(): returned[slot_index].reshape(docs_here, slot_count, hidden_width)]
  transfers between devices with their start and end apart: 9 -> 0, of which waited for: 6 -> 0; matrix products, arithmetic and copies ran while one was open for 16% -> 0% of each run, Pallas kernels for 0% -> 0%
where the time goes in v1:
time: 161 us; the launch traced here: 160 us
  Pallas kernels  154 us (96%)
  local copies, waits for them, and re-layouts  5.37 us (3%)
    pallas_call x1, Pallas kernels, fused(): pl.pallas_call(functools.partial(kernel, cap), out_shape=jax.ShapeDtypeSt...  154 us
    unnamed x2, local copies, waits for them, and re-layouts  3.34 us

profile of v1, /device:TPU:9, one launch (start us, length us, event | category | flops | bytes accessed | tf_op | source)
XLA Modules:
  0.0 160.3 jit_solution(9931148563430060524)
XLA Ops:
  0.0 0.7 divide_bitcast_fusion
  0.7 1.3 reshape.11.head_bias_ref
  2.0 0.7 copy.12.scale_ref
  2.7 1.6 copy.14
  4.3 154.3 %shard_map.100 = bf16[128,1536]{1,0:T(8,128)(2,1)} custom-call(bf16[4,128,128]{2,1,0:T(8,128)(2,1)} %bitcast.10, s32[4,128]{1,0:T(4,128)} %bitcast.14, s32[4,128]{1,0:T(4,128)} %bitcast.15, f32[128,1]{1,0:T(8,128)} %copy.12.scale_ref, bf16[1024,2048]{1,0:T(8,128)(2,1)} %weight_ref.1, f32[4,1,512]{2,1,0:T(1,128)} %bitcast.13, bf16[192,512]{1,0:T(8,128)(2,1)} %bitcast.11, ...), custom_call_target="tpu_custom_call" | custom-call | tf_op jit(solution)/shard_map/pallas_call | solution.py:293
  158.6 1.8 %copy.16 = bf16[128,1536]{1,0:T(8,128)(2,1)} copy(bf16[128,1536]{1,0:T(8,128)(2,1)} %shard_map.100) | data formatting | bytes 786432

commit v2 on v1

--- a/solution.py
+++ b/solution.py
@@ -10,8 +10,7 @@
 MESH = pl.DeviceIdType.MESH
 F32 = jnp.float32
 BF16 = jnp.bfloat16
-CHIPS = (1, 4, 5)
-CORE = 2
+X, Y, CORE = 1, 4, 2
 ORDER = (5, 7, 1, 3, 4, 6, 2)
 
 
@@ -29,15 +28,16 @@
 
 def kernel(
     cap,
-    counts_ref, owner_ref, sub_ref, scale_ref, weight_ref, bias_ref,
+    counts_ref, owner_ref, sub_ref, length_ref, weight_ref, bias_ref,
     head_ref, head_bias_ref, factor_ref, noise_ref,
     out_ref,
     cbuf, dtbuf, zin, dtin, pin, pmeta, spread, obuf, rbuf, zs, zr, own, dtp,
-    head_all, fac_all, total,
+    head_all, fac_all, total, wide,
     zc_s, zc_r, zd_s, zd_r, zw_s, zw_r, pc_s, pc_r, pm_s, pm_r,
-    ret_s, ret_r, zp_s, zp_r, wp_s, wp_r, wc_s, wc_r,
+    ret_s, ret_r, zp_s, zp_r, wp_s, wp_r,
 ):
-    slots, docs, width = counts_ref.shape
+    slots, docs = owner_ref.shape
+    width = counts_ref.shape[1]
     owners = 32
     rows = 8 * cap
     hc = head_ref.shape[1]
@@ -74,6 +74,8 @@
     place_iota = lax.broadcasted_iota(jnp.int32, (128, docs), 0)
     row_iota = lax.broadcasted_iota(jnp.int32, (rows, docs), 0)
     carry = jnp.zeros((owners, 1), F32)
+    wide[...] = counts_ref[...].astype(F32)
+    counts = [wide[pl.ds(s, docs, stride=slots), :].astype(BF16) for s in range(slots)]
     meta = jnp.zeros((64, 128), F32)
     full = []
     for s in range(slots):
@@ -95,7 +97,7 @@
         dt = jnp.zeros((rows, docs), F32)
         for s in range(slots):
             sel = jnp.where(row_iota + zo * rows == full[s], 1.0, 0.0)
-            acc = acc + nn(sel.astype(BF16), counts_ref[s])
+            acc = acc + nn(sel.astype(BF16), counts[s])
             dt = dt + sel
         cbuf[zo, 0:rows, :] = acc.astype(BF16)
         cbuf[zo, rows : rows + 16, :] = meta[zo * 16 : zo * 16 + 16, :].astype(BF16)
@@ -115,16 +117,23 @@
             rc(factor_ref, fac_all.at[v, z, x], zw_s.at[1, k], zw_r.at[1, k], zpeer(k)),
         )
 
+    def piece(t, k, r, hop):
+        j = me ^ r
+        ref = (head_all, fac_all)[t].at[j // 2, z ^ k, j % 2]
+        rel = r ^ hop
+        return rc(ref, ref, wp_s.at[t, k, rel], wp_r.at[t, k, rel], ppeer(hop))
+
+    head_all[v, z, x] = head_ref[...]
+    fac_all[v, z, x] = factor_ref[...]
     for k in (2, 3, 1):
         zc(k).start()
     for k in (2, 3, 1):
-        zd(k).start()
         for c in zw(k):
             c.start()
+    for k in (2, 3, 1):
+        zd(k).start()
     zin[0] = cbuf[z]
     dtin[0] = dtbuf[z]
-    head_all[v, z, x] = head_ref[...]
-    fac_all[v, z, x] = factor_ref[...]
 
     def pc(r):
         j = me ^ r
@@ -138,6 +147,9 @@
     for r in ORDER:
         for c in pc(r):
             c.start()
+    for t in range(2):
+        for hop in (X, Y, CORE):
+            piece(t, 0, 0, hop).start()
     pin[0] = zin[:, pl.ds(pl.multiple_of(me * cap, cap), cap), :]
     pmeta[0] = zin[:, rows : rows + 16, :]
 
@@ -181,30 +193,25 @@
 
     lax.fori_loop(0, 4, owner_chunk, 0)
 
-    def plane_copy(r):
-        dev = ppeer(r)
-        return (
-            rc(head_all.at[v, :, x], head_all.at[v, :, x], wp_s.at[0, r], wp_r.at[0, r], dev),
-            rc(fac_all.at[v, :, x], fac_all.at[v, :, x], wp_s.at[1, r], wp_r.at[1, r], dev),
-        )
-
-    def core_copy(r):
-        dev = ppeer(CORE)
-        j = me ^ r
-        vv, xx = j // 2, j % 2
-        return (
-            rc(head_all.at[vv, :, xx], head_all.at[vv, :, xx], wc_s.at[0, r], wc_r.at[0, r], dev),
-            rc(fac_all.at[vv, :, xx], fac_all.at[vv, :, xx], wc_s.at[1, r], wc_r.at[1, r], dev),
-        )
-
     for k in range(1, 4):
-        for c in zw(k):
+        for t, c in enumerate(zw(k)):
             c.wait_recv()
-    for r in CHIPS:
-        for c in plane_copy(r):
-            c.start()
-    for c in core_copy(0):
-        c.start()
+            for hop in (X, Y, CORE):
+                piece(t, k, 0, hop).start()
+
+    def second(k):
+        for t in range(2):
+            first, then = ((X, Y), (Y, X))[t]
+            piece(t, k, 0, first).wait_recv()
+            piece(t, k, first, then).start()
+            piece(t, k, first, CORE).start()
+            piece(t, k, 0, then).wait_recv()
+            piece(t, k, then, CORE).start()
+
+    def third(k):
+        for t in range(2):
+            piece(t, k, X, Y).wait_recv()
+            piece(t, k, X ^ Y, CORE).start()
 
     for k in range(1, 4):
         zd(k).wait_recv()
@@ -215,26 +222,29 @@
     def zp(h, k):
         return rc(zs.at[h, k], zr.at[h, k], zp_s.at[h, k], zp_r.at[h, k], zpeer(k))
 
-    def combine_chunk(h, _):
+    def combine_chunk(h):
         for r in range(1, 8):
             ret(h, r).wait_recv()
         for k in (2, 3, 1):
             zs[h, k] = tn(dtp[k], rbuf[h, k]).astype(BF16)
             zp(h, k).start()
         own[h] = tn(dtp[0], rbuf[h, 0])
-        return 0
-
-    lax.fori_loop(0, 4, combine_chunk, 0)
-
-    for r in CHIPS:
-        for c in plane_copy(r):
-            c.wait_recv()
-        for c in core_copy(r):
-            c.start()
-    for r in (0,) + CHIPS:
-        for c in core_copy(r):
-            c.wait_recv()
-
+
+    second(0)
+    for h in range(4):
+        combine_chunk(h)
+        third(h)
+        if h < 3:
+            second(h + 1)
+
+    for k in range(4):
+        for t in range(2):
+            for r in (0, X, Y, X ^ Y):
+                piece(t, k, r, CORE).wait_recv()
+
+    docs_eye = lax.broadcasted_iota(jnp.int32, (docs, docs), 0) == lax.broadcasted_iota(jnp.int32, (docs, docs), 1)
+    length = jnp.sum(jnp.where(docs_eye, length_ref[...].astype(F32), 0.0), axis=1, keepdims=True)
+    scale = float(128 * slots) / length
     kc = factor_ref.shape[1]
     for w in range(4):
         block = fac_all[w].reshape(-1, kc)
@@ -246,7 +256,7 @@
         summed = own[h]
         for k in range(1, 4):
             summed = summed + zr[h, k].astype(F32)
-        value = summed * scale_ref[...] + bias_ref[h]
+        value = summed * scale + bias_ref[h]
         hidden = (jnp.maximum(value, 0.0) + jnp.log1p(jnp.exp(-jnp.abs(value)))).astype(BF16)
         total[...] += nt(hidden, head_all[h].reshape(-1, hc))
         return 0
@@ -262,12 +272,14 @@
     for r in range(1, 8):
         for c in pc(r):
             c.wait_send()
-    for r in CHIPS:
-        for c in plane_copy(r):
-            c.wait_send()
-    for r in (0,) + CHIPS:
-        for c in core_copy(r):
-            c.wait_send()
+    for k in range(4):
+        for t in range(2):
+            first, then = ((X, Y), (Y, X))[t]
+            piece(t, k, 0, X).wait_send()
+            piece(t, k, 0, Y).wait_send()
+            piece(t, k, first, then).wait_send()
+            for r in (0, X, Y, X ^ Y):
+                piece(t, k, r, CORE).wait_send()
 
     def drain(h, _):
         for r in range(1, 8):
@@ -287,7 +299,6 @@
     cap = 2 * docs * slots // 32
     hc, topics = head_weight.shape[0], head_bias.shape[0]
     rows = 8 * cap
-    scale = (128.0 * slots / doc_len.astype(F32)).reshape(docs, 1)
     dma = pltpu.SemaphoreType.DMA
     kd, kc = head_weight.shape[1], factor.shape[0]
     return pl.pallas_call(
@@ -312,19 +323,20 @@
             pltpu.VMEM((4, 4, 2, kd, hc), BF16),
             pltpu.VMEM((4, 4, 2, factor.shape[1], kc), BF16),
             pltpu.VMEM((docs, topics), F32),
+            pltpu.VMEM((docs * slots, width), F32),
             dma((4,)), dma((4,)), dma((4,)), dma((4,)), dma((2, 4)), dma((2, 4)),
             dma((8,)), dma((8,)), dma((8,)), dma((8,)),
             dma((4, 8)), dma((4, 8)), dma((4, 4)), dma((4, 4)),
-            dma((2, 8)), dma((2, 8)), dma((2, 8)), dma((2, 8)),
+            dma((2, 4, 8)), dma((2, 4, 8)),
         ],
         compiler_params=pltpu.CompilerParams(
             collective_id=0, has_side_effects=True, vmem_limit_bytes=58 * 1024 * 1024
         ),
     )(
-        jnp.transpose(counts, (1, 0, 2)),
+        counts.reshape(docs * slots, width),
         doc_owner.T,
         doc_sub.T,
-        scale,
+        doc_len.reshape(1, docs),
         first_weight,
         first_bias.reshape(4, 1, hc),
         head_weight.T,

time: 161 us -> 151 us (0.938)
  Pallas kernels: 154 us -> 148 us
  local copies, waits for them, and re-layouts: 5.37 us -> 3.06 us
    pallas_call x1, Pallas kernels: 154 us -> 148 us  [fused(): pl.pallas_call(functools.partial(kernel, cap), out_shape=jax.ShapeDtypeSt...]
    unnamed x2 -> x1, local copies, waits for them, and re-layouts: 3.34 us -> 1.77 us
where the time goes in v2:
time: 151 us
  Pallas kernels  148 us (98%)
  local copies, waits for them, and re-layouts  3.06 us (2%)
    pallas_call x1, Pallas kernels, fused(): pl.pallas_call(functools.partial(kernel, cap), out_shape=jax.ShapeDtypeSt...  148 us

profile of v2, /device:TPU:9, one launch (start us, length us, event | category | flops | bytes accessed | tf_op | source)
XLA Modules:
  0.0 151.1 jit_solution(17924554875123154801)
XLA Ops:
  0.0 1.3 reshape.15.head_bias_ref
  1.3 148.1 %shard_map.100 = bf16[128,1536]{1,0:T(8,128)(2,1)} custom-call(bf16[512,128]{1,0:T(8,128)(2,1)} %bitcast.9, s32[4,128]{1,0:T(4,128)} %bitcast.11, s32[4,128]{1,0:T(4,128)} %bitcast.12, s32[1,128]{1,0:T(1,128)} %bitcast.13, bf16[1024,2048]{1,0:T(8,128)(2,1)} %weight_ref.1, f32[4,1,512]{2,1,0:T(1,128)} %bitcast.10, bf16[192,512]{1,0:T(8,128)(2,1)} %bitcast.7, ...), custom_call_target="tpu_custom_call" | custom-call | tf_op jit(solution)/shard_map/pallas_call | solution.py:304
  149.4 1.8 %copy.12 = bf16[128,1536]{1,0:T(8,128)(2,1)} copy(bf16[128,1536]{1,0:T(8,128)(2,1)} %shard_map.100) | data formatting | bytes 786432

commit v3 on v2

--- a/solution.py
+++ b/solution.py
@@ -29,10 +29,10 @@
 def kernel(
     cap,
     counts_ref, owner_ref, sub_ref, length_ref, weight_ref, bias_ref,
-    head_ref, head_bias_ref, factor_ref, noise_ref,
-    out_ref,
+    head_ref, factor_ref, noise_ref,
+    total,
     cbuf, dtbuf, zin, dtin, pin, pmeta, spread, obuf, rbuf, zs, zr, own, dtp,
-    head_all, fac_all, total, wide,
+    head_all, fac_all, wide,
     zc_s, zc_r, zd_s, zd_r, zw_s, zw_r, pc_s, pc_r, pm_s, pm_r,
     ret_s, ret_r, zp_s, zp_r, wp_s, wp_r,
 ):
@@ -127,11 +127,6 @@
     fac_all[v, z, x] = factor_ref[...]
     for k in (2, 3, 1):
         zc(k).start()
-    for k in (2, 3, 1):
-        for c in zw(k):
-            c.start()
-    for k in (2, 3, 1):
-        zd(k).start()
     zin[0] = cbuf[z]
     dtin[0] = dtbuf[z]
 
@@ -147,6 +142,11 @@
     for r in ORDER:
         for c in pc(r):
             c.start()
+    for k in (2, 3, 1):
+        for c in zw(k):
+            c.start()
+    for k in (2, 3, 1):
+        zd(k).start()
     for t in range(2):
         for hop in (X, Y, CORE):
             piece(t, 0, 0, hop).start()
@@ -233,9 +233,10 @@
     second(0)
     for h in range(4):
         combine_chunk(h)
-        third(h)
-        if h < 3:
-            second(h + 1)
+    for k in range(1, 4):
+        second(k)
+    for k in range(4):
+        third(k)
 
     for k in range(4):
         for t in range(2):
@@ -248,7 +249,7 @@
     kc = factor_ref.shape[1]
     for w in range(4):
         block = fac_all[w].reshape(-1, kc)
-        total[:, w * kc : (w + 1) * kc] = nn(noise_ref[...], block) + head_bias_ref[:, w * kc : (w + 1) * kc]
+        total[:, w * kc : (w + 1) * kc] = nn(noise_ref[...], block)
 
     def final_chunk(h, _):
         for k in range(1, 4):
@@ -262,7 +263,6 @@
         return 0
 
     lax.fori_loop(0, 4, final_chunk, 0)
-    out_ref[...] = total[...].astype(BF16)
 
     for k in range(1, 4):
         zc(k).wait_send()
@@ -301,10 +301,10 @@
     rows = 8 * cap
     dma = pltpu.SemaphoreType.DMA
     kd, kc = head_weight.shape[1], factor.shape[0]
-    return pl.pallas_call(
+    total = pl.pallas_call(
         functools.partial(kernel, cap),
-        out_shape=jax.ShapeDtypeStruct((docs, topics), BF16),
-        in_specs=[pl.BlockSpec(memory_space=pltpu.VMEM)] * 10,
+        out_shape=jax.ShapeDtypeStruct((docs, topics), F32),
+        in_specs=[pl.BlockSpec(memory_space=pltpu.VMEM)] * 9,
         out_specs=pl.BlockSpec(memory_space=pltpu.VMEM),
         scratch_shapes=[
             pltpu.VMEM((4, rows + 16, width), BF16),
@@ -322,7 +322,6 @@
             pltpu.VMEM((4, rows, docs), BF16),
             pltpu.VMEM((4, 4, 2, kd, hc), BF16),
             pltpu.VMEM((4, 4, 2, factor.shape[1], kc), BF16),
-            pltpu.VMEM((docs, topics), F32),
             pltpu.VMEM((docs * slots, width), F32),
             dma((4,)), dma((4,)), dma((4,)), dma((4,)), dma((2, 4)), dma((2, 4)),
             dma((8,)), dma((8,)), dma((8,)), dma((8,)),
@@ -340,10 +339,10 @@
         first_weight,
         first_bias.reshape(4, 1, hc),
         head_weight.T,
-        head_bias.reshape(1, -1),
         factor.T,
         noise_draw,
     )
+    return (total + head_bias).astype(BF16)
 
 
 def local(

time: 151 us -> 130 us (0.86)
  Pallas kernels: 148 us -> 128 us
  local copies, waits for them, and re-layouts: 3.06 us -> 0.01 us
  other arithmetic: 0 us -> 1.93 us
    pallas_call x1, Pallas kernels: 148 us -> 128 us  [fused(): pl.pallas_call(functools.partial(kernel, cap), out_shape=jax.ShapeDtypeSt...]
    convert_element_type x0 -> x1, other arithmetic: none -> 1.93 us  [fused(): return (total + head_bias).astype(BF16)]
    unnamed x1 -> x2, local copies, waits for them, and re-layouts: 1.77 us -> 0.01 us
where the time goes in v3:
time: 130 us; the launch traced here: 129 us
  Pallas kernels  128 us (98%)
  other arithmetic  1.93 us (1%)
    pallas_call x1, Pallas kernels, fused(): pl.pallas_call(functools.partial(kernel, cap), out_shape=jax.ShapeDtypeSt...  128 us

profile of v3, /device:TPU:9, one launch (start us, length us, event | category | flops | bytes accessed | tf_op | source)
XLA Modules:
  0.0 129.5 jit_solution(11367462285655872957)
XLA Ops:
  0.0 0.0 copy-start
  0.0 127.5 %shard_map.100 = f32[128,1536]{1,0:T(8,128)} custom-call(bf16[512,128]{1,0:T(8,128)(2,1)} %bitcast.9, s32[4,128]{1,0:T(4,128)} %bitcast.11, s32[4,128]{1,0:T(4,128)} %bitcast.12, s32[1,128]{1,0:T(1,128)} %bitcast.13, bf16[1024,2048]{1,0:T(8,128)(2,1)} %weight_ref.1, f32[4,1,512]{2,1,0:T(1,128)} %bitcast.10, bf16[192,512]{1,0:T(8,128)(2,1)} %bitcast.7, ...), custom_call_target="tpu_custom_call" | custom-call | tf_op jit(solution)/shard_map/pallas_call | solution.py:304
  127.5 0.0 copy-done
  127.5 1.9 %add_convert_fusion = bf16[128,1536]{1,0:T(8,128)(2,1)} fusion(f32[128,1536]{1,0:T(8,128)} %shard_map.100, f32[1536]{0:T(1024)S(1)} %copy-done), kind=kLoop, calls=%fused_computation | loop fusion | flops 393216 | bytes 1185792 | tf_op jit(solution)/shard_map/convert_element_type | solution.py:345
Async XLA Ops:
  0.0 127.5 %copy-start = (f32[1536]{0:T(1024)S(1)}, f32[1536]{0:T(1024)}, u32[]{:S(2)}) copy-start(f32[1536]{0:T(1024)} %param.17) | copy-start | bytes 18436

commit v4 on v3

--- a/solution.py
+++ b/solution.py
@@ -121,7 +121,25 @@
         j = me ^ r
         ref = (head_all, fac_all)[t].at[j // 2, z ^ k, j % 2]
         rel = r ^ hop
-        return rc(ref, ref, wp_s.at[t, k, rel], wp_r.at[t, k, rel], ppeer(hop))
+        return rc(ref, ref, wp_s.at[t, k, rel], wp_r.at[t, k, rel], ppeer(hop or CORE))
+
+    def guarded(t, held, act):
+        if t:
+            pl.when(held)(act)
+        else:
+            act()
+
+    def go(t, k, r, hop):
+        guarded(t, (z ^ k) <= (me ^ r) // 2, lambda: piece(t, k, r, hop).start())
+
+    def sent(t, k, r, hop):
+        guarded(t, (z ^ k) <= (me ^ r) // 2, lambda: piece(t, k, r, hop).wait_send())
+
+    def got(t, k, rel):
+        guarded(t, (z ^ k) <= (me ^ rel) // 2, lambda: piece(t, k, rel, 0).wait_recv())
+
+    def turn(t, k):
+        return (Y, X) if t or k == 3 else (X, Y)
 
     head_all[v, z, x] = head_ref[...]
     fac_all[v, z, x] = factor_ref[...]
@@ -143,13 +161,13 @@
         for c in pc(r):
             c.start()
     for k in (2, 3, 1):
-        for c in zw(k):
-            c.start()
+        for t, c in enumerate(zw(k)):
+            guarded(t, z <= v, c.start)
     for k in (2, 3, 1):
         zd(k).start()
     for t in range(2):
         for hop in (X, Y, CORE):
-            piece(t, 0, 0, hop).start()
+            go(t, 0, 0, hop)
     pin[0] = zin[:, pl.ds(pl.multiple_of(me * cap, cap), cap), :]
     pmeta[0] = zin[:, rows : rows + 16, :]
 
@@ -195,23 +213,23 @@
 
     for k in range(1, 4):
         for t, c in enumerate(zw(k)):
-            c.wait_recv()
+            guarded(t, (z ^ k) <= v, c.wait_recv)
             for hop in (X, Y, CORE):
-                piece(t, k, 0, hop).start()
+                go(t, k, 0, hop)
 
     def second(k):
         for t in range(2):
-            first, then = ((X, Y), (Y, X))[t]
-            piece(t, k, 0, first).wait_recv()
-            piece(t, k, first, then).start()
-            piece(t, k, first, CORE).start()
-            piece(t, k, 0, then).wait_recv()
-            piece(t, k, then, CORE).start()
+            first, then = turn(t, k)
+            got(t, k, first)
+            go(t, k, first, then)
+            go(t, k, first, CORE)
+            got(t, k, then)
+            go(t, k, then, CORE)
 
     def third(k):
         for t in range(2):
-            piece(t, k, X, Y).wait_recv()
-            piece(t, k, X ^ Y, CORE).start()
+            got(t, k, X ^ Y)
+            go(t, k, X ^ Y, CORE)
 
     for k in range(1, 4):
         zd(k).wait_recv()
@@ -241,15 +259,15 @@
     for k in range(4):
         for t in range(2):
             for r in (0, X, Y, X ^ Y):
-                piece(t, k, r, CORE).wait_recv()
+                got(t, k, r ^ CORE)
 
     docs_eye = lax.broadcasted_iota(jnp.int32, (docs, docs), 0) == lax.broadcasted_iota(jnp.int32, (docs, docs), 1)
     length = jnp.sum(jnp.where(docs_eye, length_ref[...].astype(F32), 0.0), axis=1, keepdims=True)
     scale = float(128 * slots) / length
     kc = factor_ref.shape[1]
     for w in range(4):
-        block = fac_all[w].reshape(-1, kc)
-        total[:, w * kc : (w + 1) * kc] = nn(noise_ref[...], block)
+        block = fac_all[w, 0 : w + 1].reshape(-1, kc)
+        total[:, w * kc : (w + 1) * kc] = nn(noise_ref[:, 0 : block.shape[0]], block)
 
     def final_chunk(h, _):
         for k in range(1, 4):
@@ -267,19 +285,19 @@
     for k in range(1, 4):
         zc(k).wait_send()
         zd(k).wait_send()
-        for c in zw(k):
-            c.wait_send()
+        for t, c in enumerate(zw(k)):
+            guarded(t, z <= v, c.wait_send)
     for r in range(1, 8):
         for c in pc(r):
             c.wait_send()
     for k in range(4):
         for t in range(2):
-            first, then = ((X, Y), (Y, X))[t]
-            piece(t, k, 0, X).wait_send()
-            piece(t, k, 0, Y).wait_send()
-            piece(t, k, first, then).wait_send()
+            first, then = turn(t, k)
+            sent(t, k, 0, X)
+            sent(t, k, 0, Y)
+            sent(t, k, first, then)
             for r in (0, X, Y, X ^ Y):
-                piece(t, k, r, CORE).wait_send()
+                sent(t, k, r, CORE)
 
     def drain(h, _):
         for r in range(1, 8):

time: 130 us -> 122 us (0.938)
  Pallas kernels: 128 us -> 119 us
    pallas_call x1, Pallas kernels: 128 us -> 119 us  [fused(): pl.pallas_call(functools.partial(kernel, cap), out_shape=jax.ShapeDtypeSt...]
where the time goes in v4:
time: 122 us; the launch traced here: 121 us
  Pallas kernels  119 us (98%)
  other arithmetic  1.93 us (2%)
    pallas_call x1, Pallas kernels, fused(): pl.pallas_call(functools.partial(kernel, cap), out_shape=jax.ShapeDtypeSt...  119 us

profile of v4, /device:TPU:9, one launch (start us, length us, event | category | flops | bytes accessed | tf_op | source)
XLA Modules:
  0.0 121.2 jit_solution(939832936129350624)
XLA Ops:
  0.0 0.0 copy-start
  0.0 119.3 %shard_map.100 = f32[128,1536]{1,0:T(8,128)} custom-call(bf16[512,128]{1,0:T(8,128)(2,1)} %bitcast.9, s32[4,128]{1,0:T(4,128)} %bitcast.11, s32[4,128]{1,0:T(4,128)} %bitcast.12, s32[1,128]{1,0:T(1,128)} %bitcast.13, bf16[1024,2048]{1,0:T(8,128)(2,1)} %weight_ref.1, f32[4,1,512]{2,1,0:T(1,128)} %bitcast.10, bf16[192,512]{1,0:T(8,128)(2,1)} %bitcast.7, ...), custom_call_target="tpu_custom_call" | custom-call | tf_op jit(solution)/shard_map/pallas_call | solution.py:322
  119.3 0.0 copy-done
  119.3 1.9 %add_convert_fusion = bf16[128,1536]{1,0:T(8,128)(2,1)} fusion(f32[128,1536]{1,0:T(8,128)} %shard_map.100, f32[1536]{0:T(1024)S(1)} %copy-done), kind=kLoop, calls=%fused_computation | loop fusion | flops 393216 | bytes 1185792 | tf_op jit(solution)/shard_map/convert_element_type | solution.py:363
Async XLA Ops:
  0.0 119.3 %copy-start = (f32[1536]{0:T(1024)S(1)}, f32[1536]{0:T(1024)}, u32[]{:S(2)}) copy-start(f32[1536]{0:T(1024)} %param.17) | copy-start | bytes 18436

commit v5 on v4

--- a/solution.py
+++ b/solution.py
@@ -32,7 +32,7 @@
     head_ref, factor_ref, noise_ref,
     total,
     cbuf, dtbuf, zin, dtin, pin, pmeta, spread, obuf, rbuf, zs, zr, own, dtp,
-    head_all, fac_all, wide,
+    head_all, fac_all, wide, hid,
     zc_s, zc_r, zd_s, zd_r, zw_s, zw_r, pc_s, pc_r, pm_s, pm_r,
     ret_s, ret_r, zp_s, zp_r, wp_s, wp_r,
 ):
@@ -256,31 +256,36 @@
     for k in range(4):
         third(k)
 
-    for k in range(4):
-        for t in range(2):
-            for r in (0, X, Y, X ^ Y):
-                got(t, k, r ^ CORE)
-
     docs_eye = lax.broadcasted_iota(jnp.int32, (docs, docs), 0) == lax.broadcasted_iota(jnp.int32, (docs, docs), 1)
     length = jnp.sum(jnp.where(docs_eye, length_ref[...].astype(F32), 0.0), axis=1, keepdims=True)
     scale = float(128 * slots) / length
-    kc = factor_ref.shape[1]
-    for w in range(4):
-        block = fac_all[w, 0 : w + 1].reshape(-1, kc)
-        total[:, w * kc : (w + 1) * kc] = nn(noise_ref[:, 0 : block.shape[0]], block)
-
-    def final_chunk(h, _):
+    def hidden_chunk(h, _):
         for k in range(1, 4):
             zp(h, k).wait_recv()
         summed = own[h]
         for k in range(1, 4):
             summed = summed + zr[h, k].astype(F32)
         value = summed * scale + bias_ref[h]
-        hidden = (jnp.maximum(value, 0.0) + jnp.log1p(jnp.exp(-jnp.abs(value)))).astype(BF16)
-        total[...] += nt(hidden, head_all[h].reshape(-1, hc))
+        hid[h] = (jnp.maximum(value, 0.0) + jnp.log1p(jnp.exp(-jnp.abs(value)))).astype(BF16)
         return 0
 
-    lax.fori_loop(0, 4, final_chunk, 0)
+    lax.fori_loop(0, 4, hidden_chunk, 0)
+
+    for t in (1, 0):
+        for k in range(4):
+            for r in (0, X, Y, X ^ Y):
+                got(t, k, r ^ CORE)
+        if t:
+            kc = factor_ref.shape[1]
+            for w in range(4):
+                block = fac_all[w, 0 : w + 1].reshape(-1, kc)
+                total[:, w * kc : (w + 1) * kc] = nn(noise_ref[:, 0 : block.shape[0]], block)
+
+    def location_chunk(h, _):
+        total[...] += nt(hid[h], head_all[h].reshape(-1, hc))
+        return 0
+
+    lax.fori_loop(0, 4, location_chunk, 0)
 
     for k in range(1, 4):
         zc(k).wait_send()
@@ -341,6 +346,7 @@
             pltpu.VMEM((4, 4, 2, kd, hc), BF16),
             pltpu.VMEM((4, 4, 2, factor.shape[1], kc), BF16),
             pltpu.VMEM((docs * slots, width), F32),
+            pltpu.VMEM((4, docs, hc), BF16),
             dma((4,)), dma((4,)), dma((4,)), dma((4,)), dma((2, 4)), dma((2, 4)),
             dma((8,)), dma((8,)), dma((8,)), dma((8,)),
             dma((4, 8)), dma((4, 8)), dma((4, 4)), dma((4, 4)),

time: 122 us -> 122 us (level)
  no operation moved by 1% of the time
where the time goes in v5:
time: 122 us; the launch traced here: 121 us
  Pallas kernels  119 us (98%)
  other arithmetic  1.93 us (2%)
    pallas_call x1, Pallas kernels, fused(): pl.pallas_call(functools.partial(kernel, cap), out_shape=jax.ShapeDtypeSt...  119 us

profile of v5, /device:TPU:9, one launch (start us, length us, event | category | flops | bytes accessed | tf_op | source)
XLA Modules:
  0.0 121.1 jit_solution(2165416360973120843)
XLA Ops:
  0.0 0.0 copy-start
  0.0 119.2 %shard_map.100 = f32[128,1536]{1,0:T(8,128)} custom-call(bf16[512,128]{1,0:T(8,128)(2,1)} %bitcast.9, s32[4,128]{1,0:T(4,128)} %bitcast.11, s32[4,128]{1,0:T(4,128)} %bitcast.12, s32[1,128]{1,0:T(1,128)} %bitcast.13, bf16[1024,2048]{1,0:T(8,128)(2,1)} %weight_ref.1, f32[4,1,512]{2,1,0:T(1,128)} %bitcast.10, bf16[192,512]{1,0:T(8,128)(2,1)} %bitcast.7, ...), custom_call_target="tpu_custom_call" | custom-call | tf_op jit(solution)/shard_map/pallas_call | solution.py:327
  119.2 0.0 copy-done
  119.2 1.9 %add_convert_fusion = bf16[128,1536]{1,0:T(8,128)(2,1)} fusion(f32[128,1536]{1,0:T(8,128)} %shard_map.100, f32[1536]{0:T(1024)S(1)} %copy-done), kind=kLoop, calls=%fused_computation | loop fusion | flops 393216 | bytes 1185792 | tf_op jit(solution)/shard_map/convert_element_type | solution.py:369
Async XLA Ops:
  0.0 119.2 %copy-start = (f32[1536]{0:T(1024)S(1)}, f32[1536]{0:T(1024)}, u32[]{:S(2)}) copy-start(f32[1536]{0:T(1024)} %param.17) | copy-start | bytes 18436
